TPU v7x, 512 devices: a whole 4x8x8 slice. The times are simulated.
512 devices in a mesh: ctx: 32 (over y, x), head: 16 (over z, core).
Axes of the slice: x: 4, y: 8, z: 8, core: 2. Of those that a mesh axis runs over, the one named last changes fastest.
Arguments:
- q_heads: bfloat16 [24576, 8192], P(('ctx', 'head')), may hold values from -16 to 16
- key_head_rows: bfloat16 [24576, 1024], P(('ctx', 'head')), may hold values from -30 to 30
- value_head_rows: bfloat16 [24576, 1024], P(('ctx', 'head')), may hold values from -6 to 6
- doc_lengths: int32 [16], replicated, may hold values from 1 to 3072, 24576 in all
Outputs:
- attended: bfloat16 [24576, 8192], P(('ctx', 'head'))
Inputs may be any that keep to these rules, and one draw needn't show every extreme that they name: `doc_lengths`: they sum to 24576; the largest is exactly 3072.
All inputs are finite; a program needn't handle non-finite values. Where the computation divides by a largest or mean magnitude, that divisor is 1e-20 or more.
Results may differ from a plain program's by a relative error of at most 0.018.
Values may be sent and summed in bfloat16 or wider, within the bound.
A program may use at most 128 MiB of HBM per device.

v0:
```python
import math

import jax
import jax.numpy as jnp
from jax import lax
from jax.sharding import PartitionSpec as P

QUERY_HEADS = 64
KEY_HEADS = 8
HEAD_SIZE = 128
TOK_CTX = 768
MOST = 3072


KCLIP = 8.0
NEG = -1e30


def passed_along(shard, axis, by):
    devices = lax.axis_size(axis)
    pairs = [(i, i + by) for i in range(devices) if 0 <= i + by < devices]
    return lax.ppermute(shard, axis, pairs)


def doc_index(positions, doc_lengths):
    ends = jnp.cumsum(doc_lengths)
    return jnp.sum((positions[:, None] >= ends[None, :]).astype(jnp.int32), axis=1)


def attend_tile(carry, queries, allowed, key_rows, value_rows):
    top_old, total_old, accum = carry
    scores = jnp.einsum("qkgd,skd->kgqs", queries, key_rows, preferred_element_type=jnp.float32)
    scores = jnp.where(allowed[None, None], scores * (1.0 / math.sqrt(HEAD_SIZE)), NEG)
    top_new = jnp.maximum(top_old, jnp.max(scores, axis=-1))
    expo = jnp.where(allowed[None, None], jnp.exp(scores - top_new[..., None]), 0.0)
    shrink = jnp.exp(top_old - top_new)
    total_new = total_old * shrink + jnp.sum(expo, axis=-1)
    contrib = jnp.einsum(
        "kgqs,skd->qkgd", expo.astype(jnp.bfloat16), value_rows, preferred_element_type=jnp.float32
    )
    accum = accum * jnp.transpose(shrink, (2, 0, 1))[..., None] + contrib
    return (top_new, total_new, accum)


def visit(carry, queries, q_pos, q_doc, key_rows, value_rows, k_pos, k_doc):
    allowed = (
        (k_pos[None, :] >= 0)
        & (k_pos[None, :] <= q_pos[:, None])
        & (k_doc[None, :] == q_doc[:, None])
    )
    return attend_tile(carry, queries, allowed, key_rows, value_rows)


def on_device(q_heads, key_head_rows, value_head_rows, doc_lengths):
    head_count = lax.axis_size("head")
    token_share = q_heads.shape[0]
    queries = q_heads.reshape(token_share, QUERY_HEADS, HEAD_SIZE)
    unscaled_keys = key_head_rows.reshape(token_share, KEY_HEADS, HEAD_SIZE)
    value_rows = value_head_rows.reshape(token_share, KEY_HEADS, HEAD_SIZE)
    head_replicas = max(head_count // KEY_HEADS, 1)
    q_local, k_local, v_local = (
        lax.all_to_all(queries, "head", split_axis=1, concat_axis=0, tiled=True),
        lax.all_to_all(
            jnp.repeat(unscaled_keys, head_replicas, axis=1),
            "head",
            split_axis=1,
            concat_axis=0,
            tiled=True,
        ),
        lax.all_to_all(
            jnp.repeat(value_rows, head_replicas, axis=1),
            "head",
            split_axis=1,
            concat_axis=0,
            tiled=True,
        ),
    )
    local_top = jnp.max(jnp.abs(k_local.astype(jnp.float32)), axis=(0, 2))
    key_scale = lax.pmax(local_top, "ctx")
    k_local = (k_local.astype(jnp.float32) * (KCLIP / key_scale)[None, :, None]).astype(
        jnp.bfloat16
    )
    tok_ctx = q_local.shape[0]
    kv_dev = k_local.shape[1]
    group_size = q_local.shape[1] // kv_dev
    q_grouped = q_local.reshape(tok_ctx, kv_dev, group_size, HEAD_SIZE)
    reach = MOST // TOK_CTX
    ctx_id = lax.axis_index("ctx")
    offsets = jnp.arange(tok_ctx, dtype=jnp.int32)
    local_pos = ctx_id * tok_ctx + offsets
    local_doc = doc_index(local_pos, doc_lengths)
    init = (
        jnp.full((kv_dev, group_size, tok_ctx), NEG, jnp.float32),
        jnp.zeros((kv_dev, group_size, tok_ctx), jnp.float32),
        jnp.zeros((tok_ctx, kv_dev, group_size, HEAD_SIZE), jnp.float32),
    )
    carry = visit(init, q_grouped, local_pos, local_doc, k_local, v_local, local_pos, local_doc)
    moving_kv = (k_local, v_local)
    for step in range(1, reach + 1):
        moving_kv = passed_along((moving_kv[0], moving_kv[1]), "ctx", 1)
        key_pos = (ctx_id - step) * tok_ctx + offsets
        carry = visit(
            carry,
            q_grouped,
            local_pos,
            local_doc,
            moving_kv[0],
            moving_kv[1],
            key_pos,
            doc_index(key_pos, doc_lengths),
        )
    top, total, accum = carry
    output = (accum / jnp.transpose(total, (2, 0, 1))[..., None]).astype(jnp.bfloat16)
    output = output.reshape(tok_ctx, kv_dev * group_size, HEAD_SIZE)
    returned = lax.all_to_all(output, "head", split_axis=0, concat_axis=1, tiled=True)
    return returned.reshape(token_share, QUERY_HEADS * HEAD_SIZE)


def solution(mesh):
    in_specs = (P(("ctx", "head"), None), P(("ctx", "head"), None), P(("ctx", "head"), None), P())
    out_specs = P(("ctx", "head"), None)
    return jax.shard_map(
        on_device, mesh=mesh, in_specs=in_specs, out_specs=out_specs, check_vma=False
    )
```

profile of v0, /device:TPU:27, one launch (start us, length us, event | category | flops | bytes accessed | tf_op | source)
XLA Modules:
  0.0 262.4 jit_solution(3975161034848572195)
XLA Ops:
  0.0 0.0 copy-start
  0.0 1.0 copy_bitcast_fusion.2
  1.0 0.7 broadcast_in_dim.132
  1.7 11.0 %all-to-all-start = ((bf16[48,16,128]{2,0,1:T(8,128)(2,1)}), bf16[48,16,128]{2,0,1:T(8,128)(2,1)S(1)}, u32[]{:S(2)}, u32[]{:S(2)}) async-start(bf16[48,16,128]{2,0,1:T(8,128)(2,1)} %bitcast.1), calls=%async_computation | async-start | bytes 393216 | tf_op jit(solution)/shard_map/all_to_all | solution.py:63
  12.7 0.5 broadcast_compare_fusion.2
  13.2 0.7 copy.47
  14.0 0.1 reduce.14
  14.1 0.9 copy_bitcast_fusion.1
  15.0 8.0 %all-to-all-done = bf16[48,16,128]{2,0,1:T(8,128)(2,1)S(1)} async-done(((bf16[48,16,128]{2,0,1:T(8,128)(2,1)}), bf16[48,16,128]{2,0,1:T(8,128)(2,1)S(1)}, u32[]{:S(2)}, u32[]{:S(2)}) %all-to-all-start) | async-done | bytes 196640 | tf_op jit(solution)/shard_map/all_to_all | solution.py:63
  23.0 0.7 broadcast_in_dim.137
  23.7 3.4 %all-to-all-start.2 = ((bf16[48,16,128]{2,0,1:T(8,128)(2,1)}), bf16[48,16,128]{2,0,1:T(8,128)(2,1)S(1)}, u32[]{:S(2)}, u32[]{:S(2)}) async-start(bf16[48,16,128]{2,0,1:T(8,128)(2,1)} %bitcast.17), calls=%async_computation.2 | async-start | bytes 393216 | tf_op jit(solution)/shard_map/all_to_all | solution.py:70
  27.1 0.0 copy-done
  27.2 1.0 copy_bitcast_fusion
  28.2 0.7 fusion.46
  28.9 53.7 %pmax.7 = f32[1]{0:T(128)} all-reduce(f32[1]{0:T(128)} %bitcast.2), channel_id=1, replica_groups=mesh['ctx'=32,'head'=16] {'ctx'}, use_global_device_ids=true, to_apply=%region_3.4 | all-reduce | flops 1 | bytes 8 | tf_op jit(solution)/shard_map/pmax | solution.py:79
  83.2 0.0 all-to-all-done.2
  83.2 20.5 %all-to-all-start.1 = ((bf16[48,64,128]{2,0,1:T(8,128)(2,1)}), bf16[48,64,128]{2,0,1:T(8,128)(2,1)}, u32[]{:S(2)}, u32[]{:S(2)}) async-start(bf16[48,64,128]{2,0,1:T(8,128)(2,1)} %copy_bitcast_fusion), calls=%async_computation.1 | async-start | bytes 1572864 | tf_op jit(solution)/shard_map/all_to_all | solution.py:62
  103.8 4.3 %collective-permute-start = (bf16[768,1,128]{2,0,1:T(8,128)(2,1)S(1)}, bf16[768,1,128]{2,0,1:T(8,128)(2,1)S(1)}, u32[]{:S(2)}, u32[]{:S(2)}) collective-permute-start(bf16[768,1,128]{2,0,1:T(8,128)(2,1)S(1)} %bitcast.384), channel_id=1, source_target_pairs={{0,16},{16,32},{32,48},{48,64},{64,80},{80,96},{96,112},{112,128},... | collective-permute-start | bytes 589832 | tf_op jit(solution)/shard_map/ppermute | solution.py:22
  108.1 4.3 %collective-permute-start.1 = (bf16[768,1,128]{2,0,1:T(8,128)(2,1)S(1)}, bf16[768,1,128]{2,0,1:T(8,128)(2,1)S(1)}, u32[]{:S(2)}, u32[]{:S(2)}) collective-permute-start(bf16[768,1,128]{2,0,1:T(8,128)(2,1)S(1)} %bitcast.386), channel_id=1, source_target_pairs={{0,16},{16,32},{32,48},{48,64},{64,80},{80,96},{96,112},{112,128},... | collective-permute-start | bytes 589832 | tf_op jit(solution)/shard_map/ppermute | solution.py:22
  112.4 0.0 collective-permute-done
  112.4 7.2 %collective-permute-start.2 = (bf16[768,1,128]{2,0,1:T(8,128)(2,1)S(1)}, bf16[768,1,128]{2,0,1:T(8,128)(2,1)S(1)}, u32[]{:S(2)}, u32[]{:S(2)}) collective-permute-start(bf16[768,1,128]{2,0,1:T(8,128)(2,1)S(1)} %collective-permute-done), channel_id=1, source_target_pairs={{0,16},{16,32},{32,48},{48,64},{64,80},{80,96},{96,112},{112,128},... | collective-permute-start | bytes 589832 | tf_op jit(solution)/shard_map/ppermute | solution.py:22
  119.7 0.0 collective-permute-done.1
  119.7 4.1 %collective-permute-start.3 = (bf16[768,1,128]{2,0,1:T(8,128)(2,1)S(1)}, bf16[768,1,128]{2,0,1:T(8,128)(2,1)S(1)}, u32[]{:S(2)}, u32[]{:S(2)}) collective-permute-start(bf16[768,1,128]{2,0,1:T(8,128)(2,1)S(1)} %collective-permute-done.1), channel_id=1, source_target_pairs={{0,16},{16,32},{32,48},{48,64},{64,80},{80,96},{96,112},{112,128},... | collective-permute-start | bytes 589832 | tf_op jit(solution)/shard_map/ppermute | solution.py:22
  123.8 0.1 convert_reduce_fusion
  123.9 0.0 collective-permute-done.2
  123.9 7.4 %collective-permute-start.4 = (bf16[768,1,128]{2,0,1:T(8,128)(2,1)S(1)}, bf16[768,1,128]{2,0,1:T(8,128)(2,1)}, u32[]{:S(2)}, u32[]{:S(2)}) collective-permute-start(bf16[768,1,128]{2,0,1:T(8,128)(2,1)S(1)} %collective-permute-done.2), channel_id=1, source_target_pairs={{0,16},{16,32},{32,48},{48,64},{64,80},{80,96},{96,112},{112,128},... | collective-permute-start | bytes 589832 | tf_op jit(solution)/shard_map/ppermute | solution.py:22
  131.4 0.0 collective-permute-done.3
  131.4 0.0 copy-start.8
  131.4 4.2 %collective-permute-start.5 = (bf16[768,1,128]{2,0,1:T(8,128)(2,1)S(1)}, bf16[768,1,128]{2,0,1:T(8,128)(2,1)}, u32[]{:S(2)}, u32[]{:S(2)}) collective-permute-start(bf16[768,1,128]{2,0,1:T(8,128)(2,1)S(1)} %collective-permute-done.3), channel_id=1, source_target_pairs={{0,16},{16,32},{32,48},{48,64},{64,80},{80,96},{96,112},{112,128},... | collective-permute-start | bytes 589832 | tf_op jit(solution)/shard_map/ppermute | solution.py:22
  135.6 0.0 copy-done.2
  135.6 0.0 copy-done.6
  135.6 0.0 copy-done.4
  135.6 5.3 %compare_and_fusion.4 = (pred[768,768]{0,1:T(8,128)(4,1)}, pred[768,768]{0,1:T(8,128)(4,1)S(1)}, pred[768,768]{0,1:T(8,128)(4,1)S(1)}, pred[768,768]{0,1:T(8,128)(4,1)S(1)}, pred[768,768]{0,1:T(8,128)(4,1)S(1)}) fusion(s32[768]{0:T(1024)S(1)} %get-tuple-element.9, s32[768]{0:T(1024)S(1)} %iota_add_fusion.4, pred[768]{0:T(1024)(128)(4,1)S(1)} %broadcast_compare_fusion.4, ...), kind=kLoop, calls=%fused_computation.44 | loop fusion | flops 11796480 | bytes 2983680 | tf_op jit(solution)/shard_map/and | solution.py:47
  140.9 0.0 collective-permute-done.4
  140.9 0.0 copy-done.8
  140.9 5.7 %collective-permute-start.6 = (bf16[768,1,128]{2,0,1:T(8,128)(2,1)}, bf16[768,1,128]{2,0,1:T(8,128)(2,1)}, u32[]{:S(2)}, u32[]{:S(2)}) collective-permute-start(bf16[768,1,128]{2,0,1:T(8,128)(2,1)} %collective-permute-done.4), channel_id=1, source_target_pairs={{0,16},{16,32},{32,48},{48,64},{64,80},{80,96},{96,112},{112,128},... | collective-permute-start | bytes 589832 | tf_op jit(solution)/shard_map/ppermute | solution.py:22
  146.6 0.0 collective-permute-done.5
  146.6 4.9 %collective-permute-start.7 = (bf16[768,1,128]{2,0,1:T(8,128)(2,1)}, bf16[768,1,128]{2,0,1:T(8,128)(2,1)}, u32[]{:S(2)}, u32[]{:S(2)}) collective-permute-start(bf16[768,1,128]{2,0,1:T(8,128)(2,1)} %collective-permute-done.5), channel_id=1, source_target_pairs={{0,16},{16,32},{32,48},{48,64},{64,80},{80,96},{96,112},{112,128},... | collective-permute-start | bytes 589832 | tf_op jit(solution)/shard_map/ppermute | solution.py:22
  151.6 0.0 all-to-all-done.1
  151.6 1.2 copy.50
  152.8 0.0 copy-start.5
  152.8 6.5 %fusion = (f32[4,768]{1,0:T(4,128)S(1)}, f32[768,768,4]{1,0,2:T(8,128)}) fusion(pred[768,768]{0,1:T(8,128)(4,1)} %get-tuple-element.21, bf16[768,128,1]{1,0,2:T(8,128)(2,1)S(1)} %bitcast.385, bf16[768,4,128]{2,0,1:T(8,128)(2,1)S(1)} %bitcast.378), kind=kOutput, calls=%fused_computation.10 | convolution fusion | flops 611054592 | bytes 11022336 | tf_op jit(solution)/shard_map/qkgd,skd->kgqs/dot_general | solution.py:32
  159.3 2.7 %fusion.3 = (f32[4,768]{1,0:T(4,128)S(1)}, f32[768,768,4]{1,0,2:T(8,128)S(1)}) fusion(pred[768,768]{0,1:T(8,128)(4,1)S(1)} %get-tuple-element.23, bf16[768,4,128]{2,0,1:T(8,128)(2,1)S(1)} %bitcast.379, bf16[768,1,128]{2,0,1:T(8,128)(2,1)} %collective-permute-done.4), kind=kOutput, calls=%fused_computation.13 | convolution fusion | flops 611054592 | bytes 11022336 | tf_op jit(solution)/shard_map/qkgd,skd->kgqs/dot_general | solution.py:32
  162.0 5.4 %fusion.2 = (f32[4,768]{1,0:T(4,128)S(1)}, f32[768,768,4]{1,0,2:T(8,128)}) fusion(pred[768,768]{0,1:T(8,128)(4,1)S(1)} %get-tuple-element.22, bf16[768,4,128]{2,0,1:T(8,128)(2,1)S(1)} %bitcast.380, bf16[768,1,128]{2,0,1:T(8,128)(2,1)S(1)} %copy-done.5), kind=kOutput, calls=%fused_computation.12 | convolution fusion | flops 611054592 | bytes 11022336 | tf_op jit(solution)/shard_map/qkgd,skd->kgqs/dot_general | solution.py:32
  167.4 0.0 copy-done.3
  167.4 5.5 %fusion.1 = (f32[4,768]{1,0:T(4,128)S(1)}, f32[768,768,4]{1,0,2:T(8,128)}) fusion(pred[768,768]{0,1:T(8,128)(4,1)S(1)} %get-tuple-element.25, bf16[768,4,128]{2,0,1:T(8,128)(2,1)S(1)} %bitcast.381, bf16[768,1,128]{2,0,1:T(8,128)(2,1)S(1)} %copy-done.3), kind=kOutput, calls=%fused_computation.11 | convolution fusion | flops 611054592 | bytes 11022336 | tf_op jit(solution)/shard_map/qkgd,skd->kgqs/dot_general | solution.py:32
  172.9 0.0 collective-permute-done.6
  172.9 2.7 %fusion.4 = (f32[4,768]{1,0:T(4,128)S(1)}, f32[768,768,4]{1,0,2:T(8,128)S(1)}) fusion(pred[768,768]{0,1:T(8,128)(4,1)S(1)} %get-tuple-element.24, bf16[768,4,128]{2,0,1:T(8,128)(2,1)S(1)} %bitcast.382, bf16[768,1,128]{2,0,1:T(8,128)(2,1)} %collective-permute-done.6), kind=kOutput, calls=%fused_computation.14 | convolution fusion | flops 611054592 | bytes 11022336 | tf_op jit(solution)/shard_map/qkgd,skd->kgqs/dot_general | solution.py:32
  175.6 0.0 copy-done.1
  175.6 6.0 %fusion.5 = f32[4,768]{1,0:T(4,128)S(1)} fusion(f32[768,768,4]{1,0,2:T(8,128)} %get-tuple-element.35, f32[4,768]{1,0:T(4,128)S(1)} %get-tuple-element.20, pred[768,768]{0,1:T(8,128)(4,1)S(1)} %copy-done.1), kind=kLoop, calls=%fused_computation.15 | loop fusion | flops 11793408 | bytes 10051584 | tf_op jit(solution)/shard_map/reduce_sum | solution.py:37
  181.6 7.9 %fusion.20 = f32[4,768,128]{2,1,0:T(8,128)} fusion(bf16[768,128,1]{1,0,2:T(8,128)(2,1)S(1)} %bitcast.387, f32[768,768,4]{1,0,2:T(8,128)} %get-tuple-element.35, f32[4,768]{1,0:T(4,128)S(1)} %get-tuple-element.20, pred[768,768]{0,1:T(8,128)(4,1)S(1)} %copy-done.1), kind=kOutput, calls=%fused_computation.30 | convolution fusion | flops 615776256 | bytes 11808768 | tf_op jit(solution)/shard_map/kgqs,skd->qkgd/dot_general | solution.py:38
  189.5 6.1 %fusion.7 = f32[4,768]{1,0:T(4,128)S(1)} fusion(f32[768,768,4]{1,0,2:T(8,128)} %get-tuple-element.33, f32[4,768]{1,0:T(4,128)S(1)} %get-tuple-element.13, pred[768,768]{0,1:T(8,128)(4,1)S(1)} %get-tuple-element.25), kind=kLoop, calls=%fused_computation.17 | loop fusion | flops 11793408 | bytes 10051584 | tf_op jit(solution)/shard_map/reduce_sum | solution.py:37
  195.6 6.0 %fusion.9 = f32[4,768]{1,0:T(4,128)S(1)} fusion(f32[768,768,4]{1,0,2:T(8,128)} %get-tuple-element.31, f32[4,768]{1,0:T(4,128)S(1)} %get-tuple-element.12, pred[768,768]{0,1:T(8,128)(4,1)S(1)} %get-tuple-element.22), kind=kLoop, calls=%fused_computation.19 | loop fusion | flops 11793408 | bytes 10051584 | tf_op jit(solution)/shard_map/reduce_sum | solution.py:37
  201.6 2.3 fusion.11
  203.9 2.3 fusion.13
  206.3 5.6 %fusion.22 = f32[4,768,128]{2,1,0:T(8,128)S(1)} fusion(f32[768,768,4]{1,0,2:T(8,128)} %get-tuple-element.33, f32[4,768]{1,0:T(4,128)S(1)} %get-tuple-element.13, pred[768,768]{0,1:T(8,128)(4,1)S(1)} %get-tuple-element.25, bf16[768,1,128]{2,0,1:T(8,128)(2,1)S(1)} %copy-done.7), kind=kOutput, calls=%fused_computation.31 | convolution fusion | flops 615776256 | bytes 11808768 | tf_op jit(solution)/shard_map/kgqs,skd->qkgd/dot_general | solution.py:38
  211.8 5.3 %fusion.24 = f32[4,768,128]{2,1,0:T(8,128)S(1)} fusion(f32[768,768,4]{1,0,2:T(8,128)} %get-tuple-element.31, f32[4,768]{1,0:T(4,128)S(1)} %get-tuple-element.12, pred[768,768]{0,1:T(8,128)(4,1)S(1)} %get-tuple-element.22, bf16[768,1,128]{2,0,1:T(8,128)(2,1)S(1)} %copy-done.9), kind=kOutput, calls=%fused_computation.32 | convolution fusion | flops 615776256 | bytes 11808768 | tf_op jit(solution)/shard_map/kgqs,skd->qkgd/dot_general | solution.py:38
  217.2 3.9 %fusion.26 = f32[4,768,128]{2,1,0:T(8,128)S(1)} fusion(f32[768,768,4]{1,0,2:T(8,128)S(1)} %get-tuple-element.29, f32[4,768]{1,0:T(4,128)S(1)} %get-tuple-element.11, pred[768,768]{0,1:T(8,128)(4,1)S(1)} %get-tuple-element.23, bf16[768,1,128]{2,0,1:T(8,128)(2,1)} %collective-permute-done.5), kind=kOutput, calls=%fused_computation.33 | convolution fusion | flops 615776256 | bytes 11808768 | tf_op jit(solution)/shard_map/kgqs,skd->qkgd/dot_general | solution.py:38
  221.1 0.0 collective-permute-done.7
  221.1 6.3 %fusion.43 = bf16[768,4,128]{2,0,1:T(8,128)(2,1)S(1)} fusion(f32[768,768,4]{1,0,2:T(8,128)S(1)} %get-tuple-element.27, f32[4,768]{1,0:T(4,128)S(1)} %get-tuple-element.10, pred[768,768]{0,1:T(8,128)(4,1)S(1)} %get-tuple-element.24, f32[4,768,128]{2,1,0:T(8,128)S(1)} %fusion.26, f32[4,768,128]{2,1,0:T(8,128)S(1)} %fusion.24, f32[4,768,128]{2,1,0:T(8,128)S(1)} %fusion.22, ...), kind=kOutput, calls=%fused_computation.56 | convolution fusion | flops 620101632 | bytes 17387520 | tf_op jit(solution)/shard_map/kgqs,skd->qkgd/dot_general | solution.py:38
  227.4 0.6 copy.57
  228.1 32.5 %all_to_all.57 = bf16[768,4,128]{2,1,0:T(4,128)(2,1)S(1)} all-to-all(bf16[768,4,128]{2,1,0:T(4,128)(2,1)S(1)} %copy.57), channel_id=1, replica_groups=mesh['ctx'=32,'head'=16] {'head'}, dimensions={0} | all-to-all | bytes 1572864 | tf_op jit(solution)/shard_map/all_to_all | solution.py:115
  260.5 0.4 copy.58
  260.9 1.5 reshape.877
  (21 shorter events, 0.2 us)
Async XLA Ops:
  0.0 27.1 %copy-start = (bf16[48,8192]{1,0:T(8,128)(2,1)S(1)}, bf16[48,8192]{1,0:T(8,128)(2,1)}, u32[]{:S(2)}) copy-start(bf16[48,8192]{1,0:T(8,128)(2,1)} %param.4) | copy-start | bytes 2359300
  1.7 21.3 %all-to-all-start = ((bf16[48,16,128]{2,0,1:T(8,128)(2,1)}), bf16[48,16,128]{2,0,1:T(8,128)(2,1)S(1)}, u32[]{:S(2)}, u32[]{:S(2)}) async-start(bf16[48,16,128]{2,0,1:T(8,128)(2,1)} %bitcast.1), calls=%async_computation | async-start | bytes 393216 | tf_op jit(solution)/shard_map/all_to_all | solution.py:63
  23.7 59.5 %all-to-all-start.2 = ((bf16[48,16,128]{2,0,1:T(8,128)(2,1)}), bf16[48,16,128]{2,0,1:T(8,128)(2,1)S(1)}, u32[]{:S(2)}, u32[]{:S(2)}) async-start(bf16[48,16,128]{2,0,1:T(8,128)(2,1)} %bitcast.17), calls=%async_computation.2 | async-start | bytes 393216 | tf_op jit(solution)/shard_map/all_to_all | solution.py:70
  83.2 68.4 %all-to-all-start.1 = ((bf16[48,64,128]{2,0,1:T(8,128)(2,1)}), bf16[48,64,128]{2,0,1:T(8,128)(2,1)}, u32[]{:S(2)}, u32[]{:S(2)}) async-start(bf16[48,64,128]{2,0,1:T(8,128)(2,1)} %copy_bitcast_fusion), calls=%async_computation.1 | async-start | bytes 1572864 | tf_op jit(solution)/shard_map/all_to_all | solution.py:62
  103.8 8.6 %collective-permute-start = (bf16[768,1,128]{2,0,1:T(8,128)(2,1)S(1)}, bf16[768,1,128]{2,0,1:T(8,128)(2,1)S(1)}, u32[]{:S(2)}, u32[]{:S(2)}) collective-permute-start(bf16[768,1,128]{2,0,1:T(8,128)(2,1)S(1)} %bitcast.384), channel_id=1, source_target_pairs={{0,16},{16,32},{32,48},{48,64},{64,80},{80,96},{96,112},{112,128},... | collective-permute-start | bytes 589832 | tf_op jit(solution)/shard_map/ppermute | solution.py:22
  108.1 11.6 %collective-permute-start.1 = (bf16[768,1,128]{2,0,1:T(8,128)(2,1)S(1)}, bf16[768,1,128]{2,0,1:T(8,128)(2,1)S(1)}, u32[]{:S(2)}, u32[]{:S(2)}) collective-permute-start(bf16[768,1,128]{2,0,1:T(8,128)(2,1)S(1)} %bitcast.386), channel_id=1, source_target_pairs={{0,16},{16,32},{32,48},{48,64},{64,80},{80,96},{96,112},{112,128},... | collective-permute-start | bytes 589832 | tf_op jit(solution)/shard_map/ppermute | solution.py:22
  112.4 23.2 %copy-start.2 = (bf16[768,1,128]{2,0,1:T(8,128)(2,1)}, bf16[768,1,128]{2,0,1:T(8,128)(2,1)S(1)}, u32[]{:S(2)}) copy-start(bf16[768,1,128]{2,0,1:T(8,128)(2,1)S(1)} %collective-permute-done) | copy-start | bytes 589828
  112.4 11.5 %collective-permute-start.2 = (bf16[768,1,128]{2,0,1:T(8,128)(2,1)S(1)}, bf16[768,1,128]{2,0,1:T(8,128)(2,1)S(1)}, u32[]{:S(2)}, u32[]{:S(2)}) collective-permute-start(bf16[768,1,128]{2,0,1:T(8,128)(2,1)S(1)} %collective-permute-done), channel_id=1, source_target_pairs={{0,16},{16,32},{32,48},{48,64},{64,80},{80,96},{96,112},{112,128},... | collective-permute-start | bytes 589832 | tf_op jit(solution)/shard_map/ppermute | solution.py:22
  119.7 15.9 %copy-start.6 = (bf16[768,1,128]{2,0,1:T(8,128)(2,1)}, bf16[768,1,128]{2,0,1:T(8,128)(2,1)S(1)}, u32[]{:S(2)}) copy-start(bf16[768,1,128]{2,0,1:T(8,128)(2,1)S(1)} %collective-permute-done.1) | copy-start | bytes 589828
  119.7 11.7 %collective-permute-start.3 = (bf16[768,1,128]{2,0,1:T(8,128)(2,1)S(1)}, bf16[768,1,128]{2,0,1:T(8,128)(2,1)S(1)}, u32[]{:S(2)}, u32[]{:S(2)}) collective-permute-start(bf16[768,1,128]{2,0,1:T(8,128)(2,1)S(1)} %collective-permute-done.1), channel_id=1, source_target_pairs={{0,16},{16,32},{32,48},{48,64},{64,80},{80,96},{96,112},{112,128},... | collective-permute-start | bytes 589832 | tf_op jit(solution)/shard_map/ppermute | solution.py:22
  123.9 11.7 %copy-start.4 = (bf16[768,1,128]{2,0,1:T(8,128)(2,1)}, bf16[768,1,128]{2,0,1:T(8,128)(2,1)S(1)}, u32[]{:S(2)}) copy-start(bf16[768,1,128]{2,0,1:T(8,128)(2,1)S(1)} %collective-permute-done.2) | copy-start | bytes 589828
  123.9 17.0 %collective-permute-start.4 = (bf16[768,1,128]{2,0,1:T(8,128)(2,1)S(1)}, bf16[768,1,128]{2,0,1:T(8,128)(2,1)}, u32[]{:S(2)}, u32[]{:S(2)}) collective-permute-start(bf16[768,1,128]{2,0,1:T(8,128)(2,1)S(1)} %collective-permute-done.2), channel_id=1, source_target_pairs={{0,16},{16,32},{32,48},{48,64},{64,80},{80,96},{96,112},{112,128},... | collective-permute-start | bytes 589832 | tf_op jit(solution)/shard_map/ppermute | solution.py:22
  131.4 9.6 %copy-start.8 = (bf16[768,1,128]{2,0,1:T(8,128)(2,1)}, bf16[768,1,128]{2,0,1:T(8,128)(2,1)S(1)}, u32[]{:S(2)}) copy-start(bf16[768,1,128]{2,0,1:T(8,128)(2,1)S(1)} %collective-permute-done.3) | copy-start | bytes 589828
  131.4 15.2 %collective-permute-start.5 = (bf16[768,1,128]{2,0,1:T(8,128)(2,1)S(1)}, bf16[768,1,128]{2,0,1:T(8,128)(2,1)}, u32[]{:S(2)}, u32[]{:S(2)}) collective-permute-start(bf16[768,1,128]{2,0,1:T(8,128)(2,1)S(1)} %collective-permute-done.3), channel_id=1, source_target_pairs={{0,16},{16,32},{32,48},{48,64},{64,80},{80,96},{96,112},{112,128},... | collective-permute-start | bytes 589832 | tf_op jit(solution)/shard_map/ppermute | solution.py:22
  140.9 32.0 %collective-permute-start.6 = (bf16[768,1,128]{2,0,1:T(8,128)(2,1)}, bf16[768,1,128]{2,0,1:T(8,128)(2,1)}, u32[]{:S(2)}, u32[]{:S(2)}) collective-permute-start(bf16[768,1,128]{2,0,1:T(8,128)(2,1)} %collective-permute-done.4), channel_id=1, source_target_pairs={{0,16},{16,32},{32,48},{48,64},{64,80},{80,96},{96,112},{112,128},... | collective-permute-start | bytes 589832 | tf_op jit(solution)/shard_map/ppermute | solution.py:22
  146.6 74.5 %collective-permute-start.7 = (bf16[768,1,128]{2,0,1:T(8,128)(2,1)}, bf16[768,1,128]{2,0,1:T(8,128)(2,1)}, u32[]{:S(2)}, u32[]{:S(2)}) collective-permute-start(bf16[768,1,128]{2,0,1:T(8,128)(2,1)} %collective-permute-done.5), channel_id=1, source_target_pairs={{0,16},{16,32},{32,48},{48,64},{64,80},{80,96},{96,112},{112,128},... | collective-permute-start | bytes 589832 | tf_op jit(solution)/shard_map/ppermute | solution.py:22
  152.8 9.3 %copy-start.5 = (bf16[768,1,128]{2,0,1:T(8,128)(2,1)S(1)}, bf16[768,1,128]{2,0,1:T(8,128)(2,1)}, u32[]{:S(2)}) copy-start(bf16[768,1,128]{2,0,1:T(8,128)(2,1)} %copy-done.4) | copy-start | bytes 589828
  159.3 8.1 %copy-start.3 = (bf16[768,1,128]{2,0,1:T(8,128)(2,1)S(1)}, bf16[768,1,128]{2,0,1:T(8,128)(2,1)}, u32[]{:S(2)}) copy-start(bf16[768,1,128]{2,0,1:T(8,128)(2,1)} %copy-done.2) | copy-start | bytes 589828
  167.4 8.2 %copy-start.1 = (pred[768,768]{0,1:T(8,128)(4,1)S(1)}, pred[768,768]{0,1:T(8,128)(4,1)}, u32[]{:S(2)}) copy-start(pred[768,768]{0,1:T(8,128)(4,1)} %get-tuple-element.21) | copy-start | bytes 1769476
  201.6 4.7 %copy-start.7 = (bf16[768,1,128]{2,0,1:T(8,128)(2,1)S(1)}, bf16[768,1,128]{2,0,1:T(8,128)(2,1)}, u32[]{:S(2)}) copy-start(bf16[768,1,128]{2,0,1:T(8,128)(2,1)} %copy-done.6) | copy-start | bytes 589828
  206.3 5.6 %copy-start.9 = (bf16[768,1,128]{2,0,1:T(8,128)(2,1)S(1)}, bf16[768,1,128]{2,0,1:T(8,128)(2,1)}, u32[]{:S(2)}) copy-start(bf16[768,1,128]{2,0,1:T(8,128)(2,1)} %copy-done.8) | copy-start | bytes 589828
  217.1 4.0 %copy-start.10 = (f32[4,768,128]{2,1,0:T(8,128)S(1)}, f32[4,768,128]{2,1,0:T(8,128)}, u32[]{:S(2)}) copy-start(f32[4,768,128]{2,1,0:T(8,128)} %fusion.20) | copy-start | bytes 4718596
where the time goes:
time: 263 us; the launch traced here: 262 us
  blocking collectives  86.1 us (33%)
  starting transfers between devices  77.1 us (29%)
  matrix products  51.7 us (20%)
  other arithmetic  29.7 us (11%)
  local copies, waits for them, and re-layouts  8.78 us (3%)
  waiting for transfers between devices  8.01 us (3%)
    pmax x1, blocking collectives, on_device(): key_scale = lax.pmax(local_top, 'ctx')  53.7 us
    ppermute x8, starting transfers between devices, passed_along(): return lax.ppermute(shard, axis, pairs)  42.1 us
    all_to_all x1, blocking collectives, on_device(): lax.all_to_all(output, 'head', split_axis=0, concat_axis=1, tiled=True)  32.5 us
    dot_general x5, matrix products, attend_tile(): jnp.einsum('kgqs,skd->qkgd', expo.astype(jnp.bfloat16), value_rows, prefe...  28.9 us
    dot_general x5, matrix products, attend_tile(): jnp.einsum('qkgd,skd->kgqs', queries, key_rows, preferred_element_type=jn...  22.8 us
    reduce_sum x5, other arithmetic, attend_tile(): total_new = total_old * shrink + jnp.sum(expo, axis=-1)  22.7 us
    all_to_all x1, starting transfers between devices, on_device(): lax.all_to_all(queries, 'head', split_axis=1, concat_axis=0, tiled=True)  20.5 us
    all_to_all x1, starting transfers between devices, on_device(): lax.all_to_all(jnp.repeat(unscaled_keys, head_replicas, axis=1), 'head',...  11 us
  transfers between devices with their start and end apart: 11, of which 1 were waited for; matrix products, arithmetic and copies ran while one was open for 30% of the time, Pallas kernels for 0%

commit v1 on v0

v1 whole, which is shorter than its diff:
```python
import math

import jax
import jax.numpy as jnp
from jax import lax
from jax.experimental import pallas as pl
from jax.experimental.pallas import tpu as pltpu
from jax.sharding import PartitionSpec as P

HEAD_SIZE = 128
KCLIP = 8.0
NEG = -1e30
MESH = pl.DeviceIdType.MESH
BF = jnp.bfloat16
F32 = jnp.float32
NX, NY, NZ = 4, 8, 8
SHARE = 48
CHIP = 2 * SHARE
BLOCK = NZ * CHIP
REACH = 4
OWN = REACH * NZ
KEYS = (REACH + 1) * BLOCK
GROUP = 4
COLS = GROUP * HEAD_SIZE
TILE = 192
TDEV = TILE // SHARE
TILES = BLOCK // TILE
ROWS = TILE * GROUP
CHUNKS = ((2304, 1024), (1536, 768), (768, 768), (0, 768))
DOCS = 16
NT = (((1,), (1,)), ((), ()))


def attend_tile(t, base, factor, ends, q_ref, k_ref, vt_ref, o_ref):
    start = pl.multiple_of((t * TILE) // 128 * 128, 128)
    rows = [q_ref[TDEV * t + d, :, HEAD_SIZE * j : HEAD_SIZE * (j + 1)] for j in range(GROUP) for d in range(TDEV)]
    queries = (jnp.concatenate(rows, axis=0).astype(F32) * factor).astype(BF)
    place = lax.rem(lax.broadcasted_iota(jnp.int32, (1, ROWS), 1), TILE)
    q_pos = base + t * TILE + place
    low = jnp.zeros((1, ROWS), jnp.int32)
    for e in ends:
        low = jnp.where(q_pos >= e, e, low)
    k_base = base - REACH * BLOCK + start
    low = low - k_base
    high = q_pos - k_base
    top = jnp.full((1, ROWS), NEG, F32)
    accum = jnp.zeros((HEAD_SIZE + 16, ROWS), F32)
    for first, size in CHUNKS:
        at = pl.multiple_of(start + first, 128)
        scores = lax.dot_general(k_ref[pl.ds(at, size), :], queries, NT, preferred_element_type=F32)
        k_row = lax.broadcasted_iota(jnp.int32, (size, ROWS), 0) + first
        allowed = k_row >= low
        if first + size > REACH * BLOCK:
            allowed = allowed & (k_row <= high)
        scores = jnp.where(allowed, scores, NEG)
        partial = jnp.max(scores.reshape(size // 8, 8, ROWS), axis=0)
        top_new = jnp.maximum(top, jnp.max(partial, axis=0, keepdims=True))
        expo = jnp.exp2(scores - top_new).astype(BF)
        contrib = jnp.dot(vt_ref[:, pl.ds(at, size)], expo, preferred_element_type=F32)
        accum = accum * jnp.exp2(top - top_new) + contrib
        top = top_new
    out = accum[:HEAD_SIZE] / accum[HEAD_SIZE : HEAD_SIZE + 1]
    out = out.T.astype(BF)
    for j in range(GROUP):
        for d in range(TDEV):
            r = (j * TDEV + d) * SHARE
            o_ref[TDEV * t + d, :, HEAD_SIZE * j : HEAD_SIZE * (j + 1)] = out[r : r + SHARE]


def kernel(
    len_ref, q_hbm, k_hbm, v_hbm, out_hbm,
    q_buf, o_buf, kv_buf, k_flat, vt, mine, tops_y, tops_x,
    q_send, q_recv, kv_send, kv_recv, y_send, y_recv, x_send, x_recv, d_send, d_recv,
    ty_send, ty_recv, tx_send, tx_recv, o_send, o_recv, local,
):
    c = lax.axis_index("ctx")
    h = lax.axis_index("head")
    x = lax.rem(c, NX)
    y = lax.div(c, NX)
    z = lax.div(h, 2)
    core = lax.rem(h, 2)
    heads = 2 * NZ

    def head_peer(k):
        return lax.rem(h + k, heads)

    def x_peer(k):
        return y * NX + lax.rem(x + k, NX)

    def y_peer(k):
        return lax.rem(y + k, NY) * NX + x

    sibling = h + 1 - 2 * core

    def remote(src, dst, send, recv, **where):
        return pltpu.make_async_remote_copy(
            src_ref=src, dst_ref=dst, send_sem=send, recv_sem=recv, device_id=where, device_id_type=MESH
        )

    barrier = pltpu.get_barrier_semaphore()
    for k in range(1, heads):
        pl.semaphore_signal(barrier, inc=1, device_id={"head": head_peer(k)}, device_id_type=MESH)
    for k in range(1, NX):
        pl.semaphore_signal(barrier, inc=1, device_id={"ctx": x_peer(k)}, device_id_type=MESH)
    for k in range(1, NY):
        pl.semaphore_signal(barrier, inc=1, device_id={"ctx": y_peer(k)}, device_id_type=MESH)
    pl.semaphore_wait(barrier, heads - 1 + NX - 1 + NY - 1)

    kv_copies = []
    for k in (1, 7, 2, 6, 3, 5, 4):
        other = lax.rem(z + k, NZ)
        lanes = pl.ds(pl.multiple_of(other * HEAD_SIZE, HEAD_SIZE), HEAD_SIZE)
        for i, source in enumerate((k_hbm, v_hbm)):
            copy = remote(
                source.at[:, lanes], kv_buf.at[i, OWN + z, core], kv_send.at[i, k], kv_recv.at[i, k], head=other * 2 + core
            )
            copy.start()
            kv_copies.append(copy)
    lanes = pl.ds(pl.multiple_of(z * HEAD_SIZE, HEAD_SIZE), HEAD_SIZE)
    kv_local = []
    for i, source in enumerate((k_hbm, v_hbm)):
        copy = pltpu.make_async_copy(source.at[:, lanes], kv_buf.at[i, OWN + z, core], local.at[i])
        copy.start()
        kv_local.append(copy)
    q_copies = []
    for k in (1, 15, 2, 14, 3, 13, 4, 12, 5, 11, 6, 10, 7, 9, 8):
        dest = head_peer(k)
        lanes = pl.ds(pl.multiple_of(dest * COLS, COLS), COLS)
        copy = remote(q_hbm.at[:, lanes], q_buf.at[h], q_send.at[k], q_recv.at[k], head=dest)
        copy.start()
        q_copies.append(copy)
    q_own = pltpu.make_async_copy(q_hbm.at[:, pl.ds(pl.multiple_of(h * COLS, COLS), COLS)], q_buf.at[h], local.at[2])
    q_own.start()

    ends = []
    total = jnp.int32(0)
    for i in range(DOCS):
        total = total + len_ref[i]
        ends.append(total)
    vt[HEAD_SIZE:, :] = jnp.ones((16, KEYS), BF)

    for copy in kv_local:
        copy.wait()
    for copy in kv_copies:
        copy.wait_recv()

    def half(i, slot):
        return kv_buf.at[i, pl.ds(slot, NZ), core]

    own_y, own_x, own_d = [], [], []
    for i in range(2):
        copy = remote(half(i, OWN), half(i, 0), y_send.at[i], y_recv.at[i], ctx=y_peer(1))
        copy.start()
        own_y.append(copy)

    def x_copy(i, k):
        slot = jnp.where(x + k < NX, OWN, 0)
        return remote(half(i, slot), half(i, OWN - k * NZ), x_send.at[i, k], x_recv.at[i, k], ctx=x_peer(k))

    for k in (1, 3, 2):
        @pl.when(x + k < NX)
        def _():
            for i in range(2):
                x_copy(i, k).start()

    def swap(i, b):
        return remote(half(i, b * NZ), half(i, b * NZ), d_send.at[i, b], d_recv.at[i, b], head=sibling)

    def flatten(b):
        k_flat[b * BLOCK : (b + 1) * BLOCK, :] = kv_buf[0, b * NZ : (b + 1) * NZ].reshape(BLOCK, HEAD_SIZE)
        values = kv_buf[1, b * NZ : (b + 1) * NZ].reshape(BLOCK, HEAD_SIZE)
        vt[:HEAD_SIZE, b * BLOCK : (b + 1) * BLOCK] = values.T

    for i in range(2):
        swap(i, REACH).start()
    for i in range(2):
        swap(i, REACH).wait_recv()

    magnitude = jnp.abs(kv_buf[0, OWN : OWN + NZ].reshape(BLOCK // 8, 8, HEAD_SIZE).astype(F32))
    mine[0] = jnp.max(magnitude, axis=0)
    y_tops = []
    for k in range(1, NY):
        copy = remote(mine.at[0], tops_y.at[k], ty_send.at[k], ty_recv.at[k], ctx=y_peer(k))
        copy.start()
        y_tops.append(copy)
    flatten(REACH)
    for copy in y_tops:
        copy.wait_recv()
    mine[1] = jnp.maximum(mine[0], jnp.max(tops_y[1:], axis=0))
    x_tops = []
    for k in range(1, NX):
        copy = remote(mine.at[1], tops_x.at[k], tx_send.at[k], tx_recv.at[k], ctx=x_peer(k))
        copy.start()
        x_tops.append(copy)

    for copy in own_y:
        copy.wait_recv()
    for k in (1, 3, 2):
        @pl.when(x + k >= NX)
        def _():
            for i in range(2):
                x_copy(i, k).start()
    for i in range(2):
        swap(i, 0).start()
    for copy in x_tops:
        copy.wait_recv()
    largest = jnp.max(jnp.maximum(mine[1], jnp.max(tops_x[1:], axis=0)))
    factor = jnp.full((1, HEAD_SIZE), KCLIP * math.log2(math.e) / math.sqrt(HEAD_SIZE), F32) / largest
    for i in range(2):
        swap(i, 0).wait_recv()
    flatten(0)
    for k in (1, 3, 2):
        for i in range(2):
            x_copy(i, k).wait_recv()
        for i in range(2):
            swap(i, REACH - k).start()
    for k in (1, 3, 2):
        for i in range(2):
            swap(i, REACH - k).wait_recv()
        flatten(REACH - k)
    q_own.wait()

    base = c * BLOCK
    own_tile = lax.div(z, 2)
    turn = 1 - 2 * lax.rem(own_tile, 2)

    def one_tile(s, carry):
        t = lax.rem(own_tile + turn * (s + 1) + TILES, TILES)
        for d in range(TDEV):
            dev = TDEV * t + d

            @pl.when(dev != h)
            def _():
                k = lax.rem(h - dev + heads, heads)
                remote(q_hbm.at[:, pl.ds(0, COLS)], q_buf.at[dev], q_send.at[k], q_recv.at[k], head=dev).wait_recv()

        attend_tile(t, base, factor, ends, q_buf, k_flat, vt, o_buf)
        lanes = pl.ds(pl.multiple_of(h * COLS, COLS), COLS)
        for d in range(TDEV):
            dev = TDEV * t + d

            @pl.when(dev != h)
            def _():
                remote(o_buf.at[dev], out_hbm.at[:, lanes], o_send.at[dev], o_recv.at[h], head=dev).start()

            @pl.when(dev == h)
            def _():
                pltpu.make_async_copy(o_buf.at[dev], out_hbm.at[:, lanes], local.at[3]).start()

        return carry

    lax.fori_loop(0, TILES, one_tile, 0)

    for copy in kv_copies + q_copies + own_y + y_tops + x_tops:
        copy.wait_send()
    for k in range(1, NX):
        for i in range(2):
            x_copy(i, k).wait_send()
    for b in range(REACH + 1):
        for i in range(2):
            swap(i, b).wait_send()
    pltpu.make_async_copy(o_buf.at[h], out_hbm.at[:, pl.ds(pl.multiple_of(h * COLS, COLS), COLS)], local.at[3]).wait()
    for k in range(1, heads):
        dev = head_peer(k)
        lanes = pl.ds(pl.multiple_of(dev * COLS, COLS), COLS)
        remote(o_buf.at[dev], out_hbm.at[:, lanes], o_send.at[dev], o_recv.at[dev], head=dev).wait()


def on_device(q, k, v, doc_lengths):
    any_space = pl.BlockSpec(memory_space=pl.ANY)
    dma = pltpu.SemaphoreType.DMA
    return pl.pallas_call(
        kernel,
        out_shape=jax.ShapeDtypeStruct(q.shape, BF),
        in_specs=[pl.BlockSpec(memory_space=pltpu.SMEM), any_space, any_space, any_space],
        out_specs=any_space,
        scratch_shapes=[
            pltpu.VMEM((2 * NZ, SHARE, COLS), BF),
            pltpu.VMEM((2 * NZ, SHARE, COLS), BF),
            pltpu.VMEM((2, OWN + NZ, 2, SHARE, HEAD_SIZE), BF),
            pltpu.VMEM((KEYS, HEAD_SIZE), BF),
            pltpu.VMEM((HEAD_SIZE + 16, KEYS), BF),
            pltpu.VMEM((2, 8, HEAD_SIZE), F32),
            pltpu.VMEM((NY, 8, HEAD_SIZE), F32),
            pltpu.VMEM((NX, 8, HEAD_SIZE), F32),
            dma((2 * NZ,)), dma((2 * NZ,)),
            dma((2, NZ)), dma((2, NZ)),
            dma((2,)), dma((2,)),
            dma((2, NX)), dma((2, NX)),
            dma((2, REACH + 1)), dma((2, REACH + 1)),
            dma((NY,)), dma((NY,)),
            dma((NX,)), dma((NX,)),
            dma((2 * NZ,)), dma((2 * NZ,)),
            dma((4,)),
        ],
        compiler_params=pltpu.CompilerParams(collective_id=0, has_side_effects=True, vmem_limit_bytes=56 << 20),
        cost_estimate=pl.CostEstimate(flops=5_200_000_000, bytes_accessed=2_000_000, transcendentals=10_000_000),
    )(doc_lengths, q, k, v)


def solution(mesh):
    rows = P(("ctx", "head"), None)
    return jax.shard_map(on_device, mesh=mesh, in_specs=(rows, rows, rows, P()), out_specs=rows, check_vma=False)
```

time: 263 us -> 73.4 us (0.28)
  the two profiles are of different devices: /device:TPU:27 before, /device:TPU:1 now
where the time goes in v1:
time: 73.4 us; the launch traced here: 73 us
  Pallas kernels  70.9 us (97%)
  local copies, waits for them, and re-layouts  2.06 us (3%)
    pallas_call x1, Pallas kernels, on_device(): pl.pallas_call(kernel, out_shape=jax.ShapeDtypeStruct(q.shape, BF), in_sp...  70.9 us
    unnamed x1, local copies, waits for them, and re-layouts  2.06 us

profile of v1, /device:TPU:1, one launch (start us, length us, event | category | flops | bytes accessed | tf_op | source)
XLA Modules:
  0.0 73.0 jit_solution(15432678925089860966)
XLA Ops:
  0.0 70.9 %shard_map.46 = bf16[48,8192]{1,0:T(8,128)(2,1)} custom-call(s32[16]{0:T(128)} %len_ref.1, bf16[48,8192]{1,0:T(8,128)(2,1)} %q_hbm.1, bf16[48,1024]{1,0:T(8,128)(2,1)} %k_hbm.1, bf16[48,1024]{1,0:T(8,128)(2,1)} %v_hbm.1), custom_call_target="tpu_custom_call" | custom-call | flops 5200000000 | bytes 2000000 | tf_op jit(solution)/shard_map/pallas_call | solution.py:272
  70.9 2.1 %copy.6 = bf16[48,8192]{1,0:T(8,128)(2,1)} copy(bf16[48,8192]{1,0:T(8,128)(2,1)} %shard_map.46) | data formatting | bytes 1572864

commit v2 on v1

v2 whole, which is shorter than its diff:
```python
import math

import jax
import jax.numpy as jnp
from jax import lax
from jax.experimental import pallas as pl
from jax.experimental.pallas import tpu as pltpu
from jax.sharding import PartitionSpec as P

HEAD_SIZE = 128
KCLIP = 8.0
NEG = -1e30
MESH = pl.DeviceIdType.MESH
BF = jnp.bfloat16
F32 = jnp.float32
NX, NY, NZ = 4, 8, 8
SHARE = 48
CHIP = 2 * SHARE
BLOCK = NZ * CHIP
REACH = 4
OWN = REACH * NZ
KEYS = (REACH + 1) * BLOCK
GROUP = 4
COLS = GROUP * HEAD_SIZE
TILE = 192
TDEV = TILE // SHARE
TILES = BLOCK // TILE
ROWS = TILE * GROUP
WINDOW = 3328
CHUNK = 256
DOCS = 16
NT = (((1,), (1,)), ((), ()))


class Tile:
    def __init__(self, t, start, base, factor, ends, q_ref):
        rows = [q_ref[TDEV * t + d, :, HEAD_SIZE * j : HEAD_SIZE * (j + 1)] for j in range(GROUP) for d in range(TDEV)]
        self.queries = (jnp.concatenate(rows, axis=0).astype(F32) * factor).astype(BF)
        place = lax.rem(lax.broadcasted_iota(jnp.int32, (1, ROWS), 1), TILE)
        q_pos = base + t * TILE + place
        low = jnp.zeros((1, ROWS), jnp.int32)
        for e in ends:
            low = jnp.where(q_pos >= e, e, low)
        k_base = base - REACH * BLOCK + start
        self.low, self.high = low - k_base, q_pos - k_base
        self.start = start
        self.top = jnp.full((1, ROWS), NEG, F32)
        self.accum = jnp.zeros((HEAD_SIZE + 16, ROWS), F32)

    def scores(self, first, k_ref):
        at = pl.ds(pl.multiple_of(self.start + first, 128), CHUNK)
        scores = lax.dot_general(k_ref[at, :], self.queries, NT, preferred_element_type=F32)
        k_row = lax.broadcasted_iota(jnp.int32, (CHUNK, ROWS), 0) + first
        allowed = k_row >= self.low
        if first + CHUNK > REACH * BLOCK:
            allowed = allowed & (k_row <= self.high)
        return jnp.where(allowed, scores, NEG)

    def visit(self, firsts, k_ref, vt_ref):
        coming = self.scores(firsts[0], k_ref)
        for n, first in enumerate(firsts):
            scores = coming
            partial = jnp.max(scores.reshape(CHUNK // 8, 8, ROWS), axis=0)
            top = jnp.maximum(self.top, jnp.max(partial, axis=0, keepdims=True))
            if n + 1 < len(firsts):
                coming = self.scores(firsts[n + 1], k_ref)
            expo = jnp.exp2(scores - top).astype(BF)
            at = pl.ds(pl.multiple_of(self.start + first, 128), CHUNK)
            contrib = jnp.dot(vt_ref[:, at], expo, preferred_element_type=F32)
            self.accum = self.accum * jnp.exp2(self.top - top) + contrib
            self.top = top

    def store(self, t, o_ref):
        out = self.accum[:HEAD_SIZE] / self.accum[HEAD_SIZE : HEAD_SIZE + 1]
        out = out.T.astype(BF)
        for j in range(GROUP):
            for d in range(TDEV):
                r = (j * TDEV + d) * SHARE
                o_ref[TDEV * t + d, :, HEAD_SIZE * j : HEAD_SIZE * (j + 1)] = out[r : r + SHARE]


def kernel(
    len_ref, q_hbm, k_hbm, v_hbm, out_hbm,
    q_buf, o_buf, kv_buf, k_flat, vt, mine, tops_y, tops_x,
    q_send, q_recv, kv_send, kv_recv, y_send, y_recv, x_send, x_recv, d_send, d_recv,
    ty_send, ty_recv, tx_send, tx_recv, o_send, o_recv, local,
):
    c = lax.axis_index("ctx")
    h = lax.axis_index("head")
    x = lax.rem(c, NX)
    y = lax.div(c, NX)
    z = lax.div(h, 2)
    core = lax.rem(h, 2)
    heads = 2 * NZ

    def head_peer(k):
        return lax.rem(h + k, heads)

    def x_peer(k):
        return y * NX + lax.rem(x + k, NX)

    def y_peer(k):
        return lax.rem(y + k, NY) * NX + x

    sibling = h + 1 - 2 * core

    def remote(src, dst, send, recv, **where):
        return pltpu.make_async_remote_copy(
            src_ref=src, dst_ref=dst, send_sem=send, recv_sem=recv, device_id=where, device_id_type=MESH
        )

    barrier = pltpu.get_barrier_semaphore()
    for k in range(1, heads):
        pl.semaphore_signal(barrier, inc=1, device_id={"head": head_peer(k)}, device_id_type=MESH)
    for k in range(1, NX):
        pl.semaphore_signal(barrier, inc=1, device_id={"ctx": x_peer(k)}, device_id_type=MESH)
        pl.semaphore_signal(barrier, inc=1, device_id={"ctx": x_peer(k), "head": sibling}, device_id_type=MESH)
    for k in range(1, NY):
        pl.semaphore_signal(barrier, inc=1, device_id={"ctx": y_peer(k)}, device_id_type=MESH)
    pl.semaphore_wait(barrier, heads - 1 + 2 * (NX - 1) + NY - 1)

    kv_copies = ([], [])
    for i, source in enumerate((k_hbm, v_hbm)):
        for k in (4, 3, 5, 2, 6, 1, 7):
            other = lax.rem(z + k, NZ)
            lanes = pl.ds(pl.multiple_of(other * HEAD_SIZE, HEAD_SIZE), HEAD_SIZE)
            copy = remote(
                source.at[:, lanes], kv_buf.at[i, OWN + z, core], kv_send.at[i, k], kv_recv.at[i, k], head=other * 2 + core
            )
            copy.start()
            kv_copies[i].append(copy)
    lanes = pl.ds(pl.multiple_of(z * HEAD_SIZE, HEAD_SIZE), HEAD_SIZE)
    kv_local = []
    for i, source in enumerate((k_hbm, v_hbm)):
        copy = pltpu.make_async_copy(source.at[:, lanes], kv_buf.at[i, OWN + z, core], local.at[i])
        copy.start()
        kv_local.append(copy)
    q_copies = []
    for k in (1, 15, 2, 14, 3, 13, 4, 12, 5, 11, 6, 10, 7, 9, 8):
        dest = head_peer(k)
        lanes = pl.ds(pl.multiple_of(dest * COLS, COLS), COLS)
        copy = remote(q_hbm.at[:, lanes], q_buf.at[h], q_send.at[k], q_recv.at[k], head=dest)
        copy.start()
        q_copies.append(copy)
    q_own = pltpu.make_async_copy(q_hbm.at[:, pl.ds(pl.multiple_of(h * COLS, COLS), COLS)], q_buf.at[h], local.at[2])
    q_own.start()

    ends = []
    total = jnp.int32(0)
    for i in range(DOCS):
        total = total + len_ref[i]
        ends.append(total)
    vt[HEAD_SIZE:, :] = jnp.ones((16, KEYS), BF)

    def half(i, slot):
        return kv_buf.at[i, pl.ds(slot, NZ), core]

    def y_copy(i):
        return remote(half(i, OWN), half(i, 0), y_send.at[i], y_recv.at[i], ctx=y_peer(1))

    def x_copy(i, k):
        slot = jnp.where(x + k < NX, OWN, 0)
        return remote(half(i, slot), half(i, OWN - k * NZ), x_send.at[i, k], x_recv.at[i, k], ctx=x_peer(k))

    def swap(i, b):
        return remote(half(i, b * NZ), half(i, b * NZ), d_send.at[i, b], d_recv.at[i, b], head=sibling)

    def flatten(b):
        for i in range(2):
            swap(i, b).wait_recv()
        k_flat[b * BLOCK : (b + 1) * BLOCK, :] = kv_buf[0, b * NZ : (b + 1) * NZ].reshape(BLOCK, HEAD_SIZE)
        values = kv_buf[1, b * NZ : (b + 1) * NZ].reshape(BLOCK, HEAD_SIZE)
        vt[:HEAD_SIZE, b * BLOCK : (b + 1) * BLOCK] = values.T

    y_tops, x_tops = [], []
    for i in range(2):
        kv_local[i].wait()
        for copy in kv_copies[i]:
            copy.wait_recv()
        y_copy(i).start()
        for k in (1, 3, 2):
            @pl.when(x + k < NX)
            def _():
                x_copy(i, k).start()
        swap(i, REACH).start()
        if i == 0:
            keys = kv_buf[0, pl.ds(OWN, NZ), core].reshape(NZ * SHARE // 8, 8, HEAD_SIZE)
            mine[0] = jnp.max(jnp.abs(keys.astype(F32)), axis=0)
            for k in range(1, NY):
                copy = remote(mine.at[0], tops_y.at[k], ty_send.at[k], ty_recv.at[k], ctx=y_peer(k))
                copy.start()
                y_tops.append(copy)
    for i in range(2):
        y_copy(i).wait_recv()
        for k in (1, 3, 2):
            @pl.when(x + k >= NX)
            def _():
                x_copy(i, k).start()
        swap(i, 0).start()
        if i == 0:
            for copy in y_tops:
                copy.wait_recv()
            mine[1] = jnp.maximum(mine[0], jnp.max(tops_y[1:], axis=0))
            for k in range(NX):
                for far in (0, 1):
                    if k + far > 0:
                        there = {"ctx": x_peer(k), "head": sibling if far else h}
                        copy = remote(mine.at[1], tops_x.at[k, far], tx_send.at[k, far], tx_recv.at[k, far], **there)
                        copy.start()
                        x_tops.append(copy)
    flatten(REACH)
    for copy in x_tops:
        copy.wait_recv()
    tops_x[0, 0] = mine[1]
    largest = jnp.max(tops_x[...])
    factor = jnp.full((1, HEAD_SIZE), KCLIP * math.log2(math.e) / math.sqrt(HEAD_SIZE), F32) / largest
    q_own.wait()

    base = c * BLOCK
    own_tile = lax.div(z, 2)
    turn = 1 - 2 * lax.rem(z, 2)

    def tile_at(s):
        return lax.rem(own_tile + turn * (s + 1) + TILES, TILES)

    def await_queries(t):
        for d in range(TDEV):
            dev = TDEV * t + d

            @pl.when(dev != h)
            def _():
                k = lax.rem(h - dev + heads, heads)
                remote(q_hbm.at[:, pl.ds(0, COLS)], q_buf.at[dev], q_send.at[k], q_recv.at[k], head=dev).wait_recv()

    def send_out(t):
        lanes = pl.ds(pl.multiple_of(h * COLS, COLS), COLS)
        for d in range(TDEV):
            dev = TDEV * t + d

            @pl.when(dev != h)
            def _():
                remote(o_buf.at[dev], out_hbm.at[:, lanes], o_send.at[dev], o_recv.at[h], head=dev).start()

            @pl.when(dev == h)
            def _():
                pltpu.make_async_copy(o_buf.at[dev], out_hbm.at[:, lanes], local.at[3]).start()

    t = tile_at(0)
    await_queries(t)
    tile = Tile(t, 0, base, factor, ends, q_buf)
    block = [b * BLOCK + n * CHUNK for b in range(REACH + 1) for n in range(BLOCK // CHUNK)]
    parts = BLOCK // CHUNK
    tile.visit(block[REACH * parts :], k_flat, vt)
    flatten(0)
    tile.visit(block[:parts], k_flat, vt)
    for k in (1, 3, 2):
        for i in range(2):
            x_copy(i, k).wait_recv()
            swap(i, REACH - k).start()
    for k in (1, 3, 2):
        b = REACH - k
        flatten(b)
        tile.visit(block[b * parts : (b + 1) * parts], k_flat, vt)
    tile.store(t, o_buf)
    send_out(t)

    def one_tile(s, carry):
        t = tile_at(s)
        await_queries(t)
        tile = Tile(t, pl.multiple_of((t * TILE) // 128 * 128, 128), base, factor, ends, q_buf)
        tile.visit(list(reversed(range(0, WINDOW, CHUNK))), k_flat, vt)
        tile.store(t, o_buf)
        send_out(t)
        return carry

    lax.fori_loop(1, TILES, one_tile, 0)

    for copy in kv_copies[0] + kv_copies[1] + q_copies + y_tops + x_tops:
        copy.wait_send()
    for i in range(2):
        y_copy(i).wait_send()
    for k in range(1, NX):
        for i in range(2):
            x_copy(i, k).wait_send()
    for b in range(REACH + 1):
        for i in range(2):
            swap(i, b).wait_send()
    pltpu.make_async_copy(o_buf.at[h], out_hbm.at[:, pl.ds(pl.multiple_of(h * COLS, COLS), COLS)], local.at[3]).wait()
    for k in range(1, heads):
        dev = head_peer(k)
        lanes = pl.ds(pl.multiple_of(dev * COLS, COLS), COLS)
        remote(o_buf.at[dev], out_hbm.at[:, lanes], o_send.at[dev], o_recv.at[dev], head=dev).wait()


def on_device(q, k, v, doc_lengths):
    any_space = pl.BlockSpec(memory_space=pl.ANY)
    dma = pltpu.SemaphoreType.DMA
    return pl.pallas_call(
        kernel,
        out_shape=jax.ShapeDtypeStruct(q.shape, BF),
        in_specs=[pl.BlockSpec(memory_space=pltpu.SMEM), any_space, any_space, any_space],
        out_specs=any_space,
        scratch_shapes=[
            pltpu.VMEM((2 * NZ, SHARE, COLS), BF),
            pltpu.VMEM((2 * NZ, SHARE, COLS), BF),
            pltpu.VMEM((2, OWN + NZ, 2, SHARE, HEAD_SIZE), BF),
            pltpu.VMEM((KEYS, HEAD_SIZE), BF),
            pltpu.VMEM((HEAD_SIZE + 16, KEYS), BF),
            pltpu.VMEM((2, 8, HEAD_SIZE), F32),
            pltpu.VMEM((NY, 8, HEAD_SIZE), F32),
            pltpu.VMEM((NX, 2, 8, HEAD_SIZE), F32),
            dma((2 * NZ,)), dma((2 * NZ,)),
            dma((2, NZ)), dma((2, NZ)),
            dma((2,)), dma((2,)),
            dma((2, NX)), dma((2, NX)),
            dma((2, REACH + 1)), dma((2, REACH + 1)),
            dma((NY,)), dma((NY,)),
            dma((NX, 2)), dma((NX, 2)),
            dma((2 * NZ,)), dma((2 * NZ,)),
            dma((4,)),
        ],
        compiler_params=pltpu.CompilerParams(collective_id=0, has_side_effects=True, vmem_limit_bytes=56 << 20),
        cost_estimate=pl.CostEstimate(flops=5_200_000_000, bytes_accessed=2_000_000, transcendentals=10_000_000),
    )(doc_lengths, q, k, v)


def solution(mesh):
    rows = P(("ctx", "head"), None)
    return jax.shard_map(on_device, mesh=mesh, in_specs=(rows, rows, rows, P()), out_specs=rows, check_vma=False)
```

time: 73.4 us -> 65.7 us (0.90)
  Pallas kernels: 70.9 us -> 63.5 us
    pallas_call x1, Pallas kernels: 70.9 us -> 63.5 us  [on_device(): pl.pallas_call(kernel, out_shape=jax.ShapeDtypeStruct(q.shape, BF), in_sp...]
where the time goes in v2:
time: 65.7 us; the launch traced here: 65.5 us
  Pallas kernels  63.5 us (97%)
  local copies, waits for them, and re-layouts  2.06 us (3%)
    pallas_call x1, Pallas kernels, on_device(): pl.pallas_call(kernel, out_shape=jax.ShapeDtypeStruct(q.shape, BF), in_sp...  63.5 us
    unnamed x1, local copies, waits for them, and re-layouts  2.06 us

profile of v2, /device:TPU:1, one launch (start us, length us, event | category | flops | bytes accessed | tf_op | source)
XLA Modules:
  0.0 65.5 jit_solution(8173003971436831763)
XLA Ops:
  0.0 63.5 %shard_map.46 = bf16[48,8192]{1,0:T(8,128)(2,1)} custom-call(s32[16]{0:T(128)} %len_ref.1, bf16[48,8192]{1,0:T(8,128)(2,1)} %q_hbm.1, bf16[48,1024]{1,0:T(8,128)(2,1)} %k_hbm.1, bf16[48,1024]{1,0:T(8,128)(2,1)} %v_hbm.1), custom_call_target="tpu_custom_call" | custom-call | flops 5200000000 | bytes 2000000 | tf_op jit(solution)/shard_map/pallas_call | solution.py:298
  63.5 2.1 %copy.6 = bf16[48,8192]{1,0:T(8,128)(2,1)} copy(bf16[48,8192]{1,0:T(8,128)(2,1)} %shard_map.46) | data formatting | bytes 1572864

commit v3 on v2

--- a/solution.py
+++ b/solution.py
@@ -71,7 +71,7 @@
             self.top = top
 
     def store(self, t, o_ref):
-        out = self.accum[:HEAD_SIZE] / self.accum[HEAD_SIZE : HEAD_SIZE + 1]
+        out = self.accum[:HEAD_SIZE] * (1.0 / self.accum[HEAD_SIZE : HEAD_SIZE + 1])
         out = out.T.astype(BF)
         for j in range(GROUP):
             for d in range(TDEV):
@@ -253,14 +253,15 @@
     tile.visit(block[REACH * parts :], k_flat, vt)
     flatten(0)
     tile.visit(block[:parts], k_flat, vt)
-    for k in (1, 3, 2):
-        for i in range(2):
-            x_copy(i, k).wait_recv()
-            swap(i, REACH - k).start()
-    for k in (1, 3, 2):
-        b = REACH - k
-        flatten(b)
-        tile.visit(block[b * parts : (b + 1) * parts], k_flat, vt)
+    for near in ((1, 3), (2,)):
+        for k in near:
+            for i in range(2):
+                x_copy(i, k).wait_recv()
+                swap(i, REACH - k).start()
+        for k in near:
+            b = REACH - k
+            flatten(b)
+            tile.visit(block[b * parts : (b + 1) * parts], k_flat, vt)
     tile.store(t, o_buf)
     send_out(t)
 

time: 65.7 us -> 66.9 us (1.018)
  Pallas kernels: 63.5 us -> 64.6 us
    pallas_call x1, Pallas kernels: 63.5 us -> 64.6 us  [on_device(): pl.pallas_call(kernel, out_shape=jax.ShapeDtypeStruct(q.shape, BF), in_sp...]
where the time goes in v3:
time: 66.9 us; the launch traced here: 66.7 us
  Pallas kernels  64.6 us (97%)
  local copies, waits for them, and re-layouts  2.06 us (3%)
    pallas_call x1, Pallas kernels, on_device(): pl.pallas_call(kernel, out_shape=jax.ShapeDtypeStruct(q.shape, BF), in_sp...  64.6 us
    unnamed x1, local copies, waits for them, and re-layouts  2.06 us

profile of v3, /device:TPU:1, one launch (start us, length us, event | category | flops | bytes accessed | tf_op | source)
XLA Modules:
  0.0 66.7 jit_solution(5879506776147861355)
XLA Ops:
  0.0 64.6 %shard_map.46 = bf16[48,8192]{1,0:T(8,128)(2,1)} custom-call(s32[16]{0:T(128)} %len_ref.1, bf16[48,8192]{1,0:T(8,128)(2,1)} %q_hbm.1, bf16[48,1024]{1,0:T(8,128)(2,1)} %k_hbm.1, bf16[48,1024]{1,0:T(8,128)(2,1)} %v_hbm.1), custom_call_target="tpu_custom_call" | custom-call | flops 5200000000 | bytes 2000000 | tf_op jit(solution)/shard_map/pallas_call | solution.py:299
  64.6 2.1 %copy.6 = bf16[48,8192]{1,0:T(8,128)(2,1)} copy(bf16[48,8192]{1,0:T(8,128)(2,1)} %shard_map.46) | data formatting | bytes 1572864
